TPU v7x, 128 devices: a whole 4x4x4 slice. The times are simulated.
128 devices in a mesh: row: 16 (over x, z_hi, core), col: 8 (over y, z_lo).
Axes of the slice: x: 4, y: 4, z: 4 (z_hi: 2, z_lo: 2; z = z_hi * 2 + z_lo), core: 2. Of those that a mesh axis runs over, the one named last changes fastest.
Arguments:
- front: float32 [48, 16, 128, 2, 8, 128], P(None, 'row', None, None, 'col')
- child_tiles: float32 [16, 8, 128, 128, 128], P('row', 'col'), may hold values from -1.5 to 1.5
- child_rows: int32 [16, 8, 128], P('row', 'col'), may hold values from 0 to 767, as said below
- child_cols: int32 [16, 8, 128], P('row', 'col'), may hold values from 0 to 15, as said below
Outputs:
- factored: float32 [48, 16, 128, 2, 8, 128], P(None, 'row', None, None, 'col')
Inputs may be any that keep to these rules, and one draw needn't show every extreme that they name: `child_rows`: parent block row of each child block. The owner of front block (i, j) is device (i mod 16, j mod 8); from one device at most 2 child blocks go to one owner, and some owners receive exactly 2 from every device. `child_cols`: parent block column of each child block, among the 2048 columns held; same owner bound as for child_rows.
All inputs are finite; a program needn't handle non-finite values.
Results may differ from a plain program's by a relative error of at most 0.00005.
Values sent between devices are 32-bit elements; how exact they have to be, the bound alone decides.
No kernel may reach another device: no remote copies, remote signals or barrier semaphores. Data moves between devices by JAX's collectives and lax.ppermute only.
A program may use at most 192 MiB of HBM per device.

v0:
```python
import jax
import jax.numpy as jnp
from jax import lax
from jax.sharding import PartitionSpec as P

CAP = 2


def broadcast(value, axis, source):
    kept = jnp.where(lax.axis_index(axis) == source, value, 0).astype(value.dtype)
    return lax.psum(kept, axis)


def factor_of(corner):
    return jnp.linalg.cholesky(0.5 * (corner + corner.T))


def solve_panel(factor, column):
    row_blocks, tile_size = (column.shape[0], column.shape[1])
    flattened = column.reshape(-1, tile_size)
    solved = jax.scipy.linalg.solve_triangular(factor, flattened.T, lower=True).T
    return solved.reshape(row_blocks, tile_size, tile_size)


def per_device(front, child_tiles, child_rows, child_cols):
    row_count = lax.axis_size("row")
    col_count = lax.axis_size("col")
    row_index = lax.axis_index("row")
    col_index = lax.axis_index("col")
    row_blocks, tile_size, col_blocks = (front.shape[0], front.shape[2], front.shape[3])
    local_front = front.reshape(row_blocks, tile_size, col_blocks, tile_size)
    flat_tiles = child_tiles.reshape(-1, tile_size, tile_size)
    parent_rows = child_rows.reshape(-1)
    parent_cols = child_cols.reshape(-1)
    devices = row_count * col_count
    slot_total = devices * CAP
    owners = parent_rows % row_count * col_count + parent_cols % col_count
    one_hot = (owners[:, None] == jnp.arange(devices, dtype=jnp.int32)[None, :]).astype(jnp.int32)
    before = jnp.sum(jnp.cumsum(one_hot, axis=0) * one_hot, axis=1) - 1
    send_slot = owners * CAP + before
    target = parent_rows // row_count * col_blocks + parent_cols // col_count
    send_tiles = (
        jnp.zeros((slot_total, tile_size, tile_size), jnp.float32).at[send_slot].set(flat_tiles)
    )
    send_index = jnp.full((slot_total,), -1, jnp.int32).at[send_slot].set(target)
    arrived_tiles, arrived_index = (
        lax.all_to_all(send_tiles, ("row", "col"), split_axis=0, concat_axis=0, tiled=True),
        lax.all_to_all(send_index, ("row", "col"), split_axis=0, concat_axis=0, tiled=True),
    )
    selector = (
        arrived_index[None, :] == jnp.arange(row_blocks * col_blocks, dtype=jnp.int32)[:, None]
    ).astype(jnp.float32)
    selector = selector.reshape(row_blocks, col_blocks, slot_total)
    assembled = local_front + jnp.einsum(
        "ams,spq->apmq", selector, arrived_tiles, precision=lax.Precision.HIGHEST
    )
    column = assembled[:, :, 0, :]
    corner = broadcast(column[0], "row", 0)
    panel_rows = solve_panel(factor_of(corner), column)
    panel_rows = broadcast(panel_rows, "col", 0)
    window_blocks = col_blocks * col_count // row_count
    window = lax.all_gather(panel_rows[:window_blocks][:, None], "row", axis=1, tiled=True)
    window = window.reshape(col_blocks, col_count, tile_size, tile_size)
    own_window = lax.dynamic_index_in_dim(window, col_index, axis=1, keepdims=False)
    update = jnp.einsum("apk,mqk->apmq", panel_rows, own_window, precision=lax.Precision.HIGHEST)
    global_rows = (jnp.arange(row_blocks, dtype=jnp.int32) * row_count + row_index)[
        :, None, None, None
    ]
    global_cols = (jnp.arange(col_blocks, dtype=jnp.int32) * col_count + col_index)[
        None, None, :, None
    ]
    result = assembled - jnp.where(global_rows > 0, update, jnp.zeros_like(update))
    result = jnp.where(global_cols == 0, panel_rows[:, :, None, :], result)
    return result.reshape(front.shape)


def solution(mesh):
    in_specs = (
        P(None, "row", None, None, "col", None),
        P("row", "col", None, None, None),
        P("row", "col", None),
        P("row", "col", None),
    )
    out_specs = P(None, "row", None, None, "col", None)
    return jax.shard_map(
        per_device, mesh=mesh, in_specs=in_specs, out_specs=out_specs, check_vma=False
    )
```

profile of v0, /device:TPU:1, one launch (start us, length us, event | category | flops | bytes accessed | tf_op | source)
XLA Modules:
  0.0 712.7 jit_solution(14597959788341730785)
XLA Ops:
  8.4 1.0 scatter_custom_fusion.1
  10.1 11.5 %all-to-all-start.1 = ((s32[128,2,1]{1,2,0:T(1,128)}), s32[128,2,1]{1,2,0:T(1,128)S(1)}, u32[]{:S(2)}, u32[]{:S(2)}) async-start(s32[128,2,1]{1,2,0:T(1,128)} %bitcast.9), calls=%async_computation.1 | async-start | bytes 131072 | tf_op jit(solution)/shard_map/all_to_all | solution.py:48
  21.6 7.8 %broadcast_in_dim.58 = f32[256,128,128]{2,1,0:T(8,128)} broadcast(f32[]{:T(128)} %constant.112.clone.1), dimensions={} | broadcast | bytes 16777220 | tf_op jit(solution)/shard_map/broadcast_in_dim | solution.py:43
  29.5 23.4 %scatter_fusion = f32[256,128,128]{2,1,0:T(8,128)} fusion(f32[256,128,128]{2,1,0:T(8,128)} %broadcast_in_dim.58, s32[128]{0:T(128)S(1)} %fusion.26, f32[128,128,128]{2,1,0:T(8,128)} %bitcast.97), kind=kCustom, calls=%fused_computation | custom fusion | bytes 25166336 | tf_op jit(solution)/shard_map/scatter | solution.py:43
  52.8 10.3 %all-to-all-start = ((f32[256,128,128]{2,1,0:T(8,128)}), f32[256,128,128]{2,1,0:T(8,128)}, u32[]{:S(2)}, u32[]{:S(2)}) async-start(f32[256,128,128]{2,1,0:T(8,128)} %scatter_fusion), calls=%async_computation | async-start | bytes 33554432 | tf_op jit(solution)/shard_map/all_to_all | solution.py:47
  63.3 14.1 %copy.25 = f32[48,1,128,2,1,128]{2,5,3,0,4,1:T(8,128)} copy(f32[48,1,128,2,1,128]{5,4,3,2,1,0:T(1,128)} %param.4) | data formatting | bytes 12582912 | tf_op args[0]
  77.9 0.8 reduce.9
  78.9 209.0 %all-to-all-done = f32[256,128,128]{2,1,0:T(8,128)} async-done(((f32[256,128,128]{2,1,0:T(8,128)}), f32[256,128,128]{2,1,0:T(8,128)}, u32[]{:S(2)}, u32[]{:S(2)}) %all-to-all-start) | async-done | bytes 16777248 | tf_op jit(solution)/shard_map/all_to_all | solution.py:47
  287.9 22.8 %fusion = f32[128,128,48,2]{1,2,3,0:T(8,128)} fusion(f32[256,128,128,1]{2,1,0,3:T(8,128)} %bitcast.8, s32[48,2]{0,1:T(2,128)S(1)} %multiply_add_fusion, s32[256]{0:T(256)S(1)} %eq.57), kind=kOutput, calls=%fused_computation.2 | convolution fusion | flops 4831862784 | bytes 23070080 | tf_op jit(solution)/shard_map/ams,spq->apmq/dot_general | solution.py:54
  310.7 6.6 copy.28
  317.3 5.9 bitcast_add_fusion
  323.2 2.7 copy-done
  326.9 131.3 %all-reduce.3.cloned.1.call-done = f32[128,128]{0,1:T(8,128)} async-done(((f32[128,128]{0,1:T(8,128)}), f32[128,128]{0,1:T(8,128)}) %all-reduce.3.cloned.1.call-update) | async-done | bytes 65552 | tf_op jit(solution)/shard_map/psum | solution.py:11
  458.2 0.9 copy.29
  459.1 0.9 fusion.16
  460.1 11.7 %cholesky.15 = f32[128,128]{1,0:T(8,128)S(1)} custom-call(f32[128,128]{1,0:T(8,128)S(1)} %fusion.15), custom_call_target="Cholesky" | custom-call | tf_op jit(solution)/shard_map/jit(cholesky)/cholesky | solution.py:15
  473.3 9.8 %custom-call.7 = f32[1,128,128]{1,2,0:T(8,128)S(1)} custom-call(f32[1,128,128]{2,1,0:T(8,128)S(1)} %fusion.12), custom_call_target="InvertDiagBlocksLowerTriangular" | custom-call | tf_op jit(solution)/shard_map/jit(_solve_triangular)/triangular_solve | solution.py:21
  483.1 7.9 %fusion.7 = f32[48,128,128]{2,1,0:T(8,128)} fusion(f32[48,128,2,128]{1,3,2,0:T(8,128)} %copy-done, pred[]{:T(512)S(6)} %eq.53, f32[1,128,128]{1,2,0:T(8,128)S(1)} %custom-call.7), kind=kOutput, calls=%fused_computation.10 | convolution fusion | flops 1208745984 | bytes 6356993 | tf_op jit(solution)/shard_map/jit(_solve_triangular)/triangular_solve | solution.py:21
  491.3 141.6 %all-reduce.5.cloned.1.call-done = f32[48,128,128]{2,1,0:T(8,128)} async-done(((f32[48,128,128]{2,1,0:T(8,128)}), f32[48,128,128]{2,1,0:T(8,128)}) %all-reduce.5.cloned.1.call-update) | async-done | bytes 3145744 | tf_op jit(solution)/shard_map/psum | solution.py:11
  632.9 1.6 slice.28
  634.6 3.7 copy.33
  638.3 44.0 %all-gather.3.cloned.1.call-done = f32[16,128,128]{2,1,0:T(8,128)} async-done(((f32[1,128,128]{2,1,0:T(8,128)}), f32[16,128,128]{2,1,0:T(8,128)}) %all-gather.3.cloned.1.call-update) | async-done | bytes 1048592 | tf_op jit(solution)/shard_map/all_gather | solution.py:62
  682.3 9.8 %select_bitcast_fusion = f32[48,1,128,2,1,128]{2,5,3,0,4,1:T(8,128)} fusion(f32[48,128,2,128]{1,3,2,0:T(8,128)} %copy-done, f32[48,128,128]{1,2,0:T(8,128)} %copy.33, pred[48]{0:T(512)(128)(4,1)S(1)} %add_compare_fusion, pred[2]{0:T(512)(128)(4,1)S(1)} %add_compare_fusion.1, f32[48,128,128]{2,1,0:T(8,128)S(1)} %copy-done.1, f32[2,8,128,128]{3,2,1,0:T(8,128)} %bitcast.98, ...), kind=kOutput, calls=%fused_computation.5 | convolution fusion | flops 2420637696 | bytes 19005494 | tf_op jit(solution)/shard_map/apk,mqk->apmq/dot_general | solution.py:65
  692.1 14.1 %copy.36 = f32[48,1,128,2,1,128]{5,4,3,2,1,0:T(1,128)} copy(f32[48,1,128,2,1,128]{2,5,3,0,4,1:T(8,128)} %select_bitcast_fusion) | data formatting | bytes 12582912 | tf_op jit(solution)/shard_map/reshape | solution.py:74
  (27 shorter events, 6.3 us)
Async XLA Ops:
  10.1 42.7 %all-to-all-start.1 = ((s32[128,2,1]{1,2,0:T(1,128)}), s32[128,2,1]{1,2,0:T(1,128)S(1)}, u32[]{:S(2)}, u32[]{:S(2)}) async-start(s32[128,2,1]{1,2,0:T(1,128)} %bitcast.9), calls=%async_computation.1 | async-start | bytes 131072 | tf_op jit(solution)/shard_map/all_to_all | solution.py:48
  52.8 235.1 %all-to-all-start = ((f32[256,128,128]{2,1,0:T(8,128)}), f32[256,128,128]{2,1,0:T(8,128)}, u32[]{:S(2)}, u32[]{:S(2)}) async-start(f32[256,128,128]{2,1,0:T(8,128)} %scatter_fusion), calls=%async_computation | async-start | bytes 33554432 | tf_op jit(solution)/shard_map/all_to_all | solution.py:47
  63.1 395.1 %all-reduce.3.cloned.1.call-start = ((), (), s32[]{:S(2)}) async-start(), calls=%async_computation.2 | async-start | bytes 131072 | tf_op jit(solution)/shard_map/psum | solution.py:11
  323.2 2.7 copy-start
  326.6 306.3 %all-reduce.5.cloned.1.call-start = ((), (), s32[]{:S(2)}) async-start(), calls=%async_computation.3 | async-start | bytes 6291456 | tf_op jit(solution)/shard_map/psum | solution.py:11
  491.0 191.3 %all-gather.3.cloned.1.call-start = ((), (), s32[]{:S(2)}) async-start(), calls=%async_computation.4 | async-start | bytes 1114112 | tf_op jit(solution)/shard_map/all_gather | solution.py:62
  632.9 49.3 %copy-start.1 = (f32[48,128,128]{2,1,0:T(8,128)S(1)}, f32[48,128,128]{2,1,0:T(8,128)}, u32[]{:S(2)}) copy-start(f32[48,128,128]{2,1,0:T(8,128)} %all-reduce.5.cloned.1.call-done) | copy-start | bytes 9437188
Sparse Core Ops, SparseCore 0:
  326.7 131.4 all-reduce.2
  491.1 141.7 all-reduce.4
  635.6 46.6 all-gather.2
where the time goes:
time: 714 us; the launch traced here: 713 us
  waiting for transfers between devices  526 us (74%)
  local copies, waits for them, and re-layouts  77.4 us (11%)
  matrix products  40.4 us (6%)
  other arithmetic  33 us (5%)
  starting transfers between devices  22.6 us (3%)
  between operations  13.2 us (2%)
    psum x2, waiting for transfers between devices, broadcast(): return lax.psum(kept, axis)  273 us
    all_to_all x1, waiting for transfers between devices, per_device(): lax.all_to_all(send_tiles, ('row', 'col'), split_axis=0, concat_axis=0, t...  209 us
    all_gather x1, waiting for transfers between devices, per_device(): lax.all_gather(panel_rows[:window_blocks][:, None], 'row', axis=1, tiled=...  44 us
    scatter x1, local copies, waits for them, and re-layouts, per_device(): jnp.zeros((slot_total, tile_size, tile_size), jnp.float32).at[send_slot]  23.4 us
    dot_general x1, matrix products, per_device(): jnp.einsum('ams,spq->apmq', selector, arrived_tiles, precision=lax.Precis...  22.8 us
    unnamed x5, local copies, waits for them, and re-layouts  16.8 us
  transfers between devices with their start and end apart: 5, of which 4 were waited for; matrix products, arithmetic and copies ran while one was open for 7% of the time, Pallas kernels for 0%

commit v1 on v0

--- a/solution.py
+++ b/solution.py
@@ -8,7 +8,7 @@
 
 def broadcast(value, axis, source):
     kept = jnp.where(lax.axis_index(axis) == source, value, 0).astype(value.dtype)
-    return lax.psum(kept, axis)
+    return jnp.sum(lax.all_gather(kept, axis), axis=0)
 
 
 def factor_of(corner):

time: 714 us -> 961 us (1.35)
  waiting for transfers between devices: 526 us -> 802 us
  local copies, waits for them, and re-layouts: 77.4 us -> 44.5 us
  other arithmetic: 33 us -> 43.9 us
    all_gather x0 -> x2, waiting for transfers between devices: none -> 533 us  [broadcast(): return jnp.sum(lax.all_gather(kept, axis), axis=0)]
    psum x2 -> x0, waiting for transfers between devices: 273 us -> none  [broadcast(): return lax.psum(kept, axis)]
    unnamed x5 -> x2, local copies, waits for them, and re-layouts: 16.8 us -> 2.7 us
    all_to_all x1, waiting for transfers between devices: 209 us -> 223 us  [per_device(): lax.all_to_all(send_tiles, ('row', 'col'), split_axis=0, concat_axis=0, t...]
    reduce_sum x0 -> x2, other arithmetic: none -> 10.9 us  [broadcast(): return jnp.sum(lax.all_gather(kept, axis), axis=0)]
  transfers between devices with their start and end apart: 5 -> 5, of which waited for: 4 -> 4; matrix products, arithmetic and copies ran while one was open for 7% -> 3% of each run, Pallas kernels for 0% -> 0%
where the time goes in v1:
time: 961 us
  waiting for transfers between devices  802 us (83%)
  local copies, waits for them, and re-layouts  44.5 us (5%)
  other arithmetic  43.9 us (5%)
  matrix products  34.8 us (4%)
  starting transfers between devices  22.1 us (2%)
  between operations  13.3 us (1%)
    all_gather x2, waiting for transfers between devices, broadcast(): return jnp.sum(lax.all_gather(kept, axis), axis=0)  533 us
    all_to_all x1, waiting for transfers between devices, per_device(): lax.all_to_all(send_tiles, ('row', 'col'), split_axis=0, concat_axis=0, t...  223 us
    all_gather x1, waiting for transfers between devices, per_device(): lax.all_gather(panel_rows[:window_blocks][:, None], 'row', axis=1, tiled=...  46.6 us
    scatter x1, local copies, waits for them, and re-layouts, per_device(): jnp.zeros((slot_total, tile_size, tile_size), jnp.float32).at[send_slot]  23.4 us
    dot_general x1, matrix products, per_device(): jnp.einsum('ams,spq->apmq', selector, arrived_tiles, precision=lax.Precis...  21.7 us
  transfers between devices with their start and end apart: 5, of which 4 were waited for; matrix products, arithmetic and copies ran while one was open for 3% of the time, Pallas kernels for 0%

profile of v1, /device:TPU:1, one launch (start us, length us, event | category | flops | bytes accessed | tf_op | source)
XLA Modules:
  0.0 960.7 jit_solution(5492700819744389999)
XLA Ops:
  7.7 0.7 fusion.25
  8.4 1.0 scatter_custom_fusion.1
  9.3 0.8 all_to_all.10
  10.1 11.5 %all-to-all-start.1 = ((s32[128,2,1]{1,2,0:T(1,128)}), s32[128,2,1]{1,2,0:T(1,128)S(1)}, u32[]{:S(2)}, u32[]{:S(2)}) async-start(s32[128,2,1]{1,2,0:T(1,128)} %bitcast.9), calls=%async_computation.1 | async-start | bytes 131072 | tf_op jit(solution)/shard_map/all_to_all | solution.py:48
  21.6 7.8 broadcast_in_dim.56
  29.5 23.4 %scatter_fusion = f32[256,128,128]{2,1,0:T(8,128)} fusion(f32[256,128,128]{2,1,0:T(8,128)} %broadcast_in_dim.56, s32[128]{0:T(128)S(1)} %fusion.25, f32[128,128,128]{2,1,0:T(8,128)} %bitcast.95), kind=kCustom, calls=%fused_computation | custom fusion | bytes 25166336 | tf_op jit(solution)/shard_map/scatter | solution.py:43
  52.8 10.3 %all-to-all-start = ((f32[256,128,128]{2,1,0:T(8,128)}), f32[256,128,128]{2,1,0:T(8,128)}, u32[]{:S(2)}, u32[]{:S(2)}) async-start(f32[256,128,128]{2,1,0:T(8,128)} %scatter_fusion), calls=%async_computation | async-start | bytes 33554432 | tf_op jit(solution)/shard_map/all_to_all | solution.py:47
  63.9 0.8 reduce.10
  64.8 223.1 %all-to-all-done = f32[256,128,128]{2,1,0:T(8,128)} async-done(((f32[256,128,128]{2,1,0:T(8,128)}), f32[256,128,128]{2,1,0:T(8,128)}, u32[]{:S(2)}, u32[]{:S(2)}) %all-to-all-start) | async-done | bytes 16777248 | tf_op jit(solution)/shard_map/all_to_all | solution.py:47
  287.9 21.7 %fusion = f32[128,128,48,2]{1,2,3,0:T(8,128)S(1)} fusion(f32[256,128,128,1]{2,1,0,3:T(8,128)} %bitcast.8, s32[48,2]{0,1:T(2,128)S(1)} %multiply_add_fusion, s32[256]{0:T(256)S(1)} %eq.57), kind=kOutput, calls=%fused_computation.2 | convolution fusion | flops 4831862784 | bytes 23070080 | tf_op jit(solution)/shard_map/ams,spq->apmq/dot_general | solution.py:54
  309.6 6.7 bitcast_add_fusion
  316.4 2.7 copy-done
  319.8 51.2 %all-gather.7.cloned.1.call-done = f32[16,128,1,128]{3,1,2,0:T(8,128)} async-done(((f32[1,128,1,128]{3,1,2,0:T(8,128)}), f32[16,128,1,128]{3,1,2,0:T(8,128)}) %all-gather.7.cloned.1.call-update) | async-done | bytes 1048592 | tf_op jit(solution)/shard_map/all_gather | solution.py:11
  371.0 1.3 reduce_sum.28
  372.4 11.7 %cholesky.16 = f32[128,128]{1,0:T(8,128)S(1)} custom-call(f32[128,128]{1,0:T(8,128)S(1)} %fusion.15), custom_call_target="Cholesky" | custom-call | tf_op jit(solution)/shard_map/jit(cholesky)/cholesky | solution.py:15
  384.1 0.7 compare_reduce_fusion
  384.8 0.7 fusion.12
  385.6 9.8 %custom-call.7 = f32[1,128,128]{1,2,0:T(8,128)S(1)} custom-call(f32[1,128,128]{2,1,0:T(8,128)S(1)} %fusion.12), custom_call_target="InvertDiagBlocksLowerTriangular" | custom-call | tf_op jit(solution)/shard_map/jit(_solve_triangular)/triangular_solve | solution.py:21
  395.4 5.4 fusion.7
  400.9 481.3 %all-gather.9.cloned.1.call-done = f32[384,128,128]{2,1,0:T(8,128)} async-done(((f32[48,128,128]{2,1,0:T(8,128)}), f32[384,128,128]{2,1,0:T(8,128)}) %all-gather.9.cloned.1.call-update) | async-done | bytes 25165840 | tf_op jit(solution)/shard_map/all_gather | solution.py:11
  882.2 9.6 %reduce_sum.29 = f32[48,128,128]{2,1,0:T(8,128)S(1)} reduce(f32[8,48,128,128]{3,2,1,0:T(8,128)} %bitcast.94, f32[]{:T(128)} %constant.114.clone.1), dimensions={0}, to_apply=%region_7.8 | reduce | flops 5505024 | bytes 28311556 | tf_op jit(solution)/shard_map/reduce_sum | solution.py:11
  892.5 46.6 %all-gather.11.cloned.1.call-done = f32[16,128,128]{2,1,0:T(8,128)} async-done(((f32[1,128,128]{2,1,0:T(8,128)}), f32[16,128,128]{2,1,0:T(8,128)}) %all-gather.11.cloned.1.call-update) | async-done | bytes 1048592 | tf_op jit(solution)/shard_map/all_gather | solution.py:62
  939.0 7.6 select_bitcast_fusion
  946.7 7.5 copy.45
  (22 shorter events, 3.5 us)
Async XLA Ops:
  10.1 42.7 %all-to-all-start.1 = ((s32[128,2,1]{1,2,0:T(1,128)}), s32[128,2,1]{1,2,0:T(1,128)S(1)}, u32[]{:S(2)}, u32[]{:S(2)}) async-start(s32[128,2,1]{1,2,0:T(1,128)} %bitcast.9), calls=%async_computation.1 | async-start | bytes 131072 | tf_op jit(solution)/shard_map/all_to_all | solution.py:48
  52.8 235.1 %all-to-all-start = ((f32[256,128,128]{2,1,0:T(8,128)}), f32[256,128,128]{2,1,0:T(8,128)}, u32[]{:S(2)}, u32[]{:S(2)}) async-start(f32[256,128,128]{2,1,0:T(8,128)} %scatter_fusion), calls=%async_computation | async-start | bytes 33554432 | tf_op jit(solution)/shard_map/all_to_all | solution.py:47
  63.1 307.9 %all-gather.7.cloned.1.call-start = ((), (), s32[]{:S(2)}) async-start(), calls=%async_computation.2 | async-start | bytes 1114112 | tf_op jit(solution)/shard_map/all_gather | solution.py:11
  316.4 2.7 copy-start
  319.7 562.5 %all-gather.9.cloned.1.call-start = ((), (), s32[]{:S(2)}) async-start(), calls=%async_computation.3 | async-start | bytes 28311552 | tf_op jit(solution)/shard_map/all_gather | solution.py:11
  400.8 538.2 %all-gather.11.cloned.1.call-start = ((), (), s32[]{:S(2)}) async-start(), calls=%async_computation.4 | async-start | bytes 1114112 | tf_op jit(solution)/shard_map/all_gather | solution.py:62
Sparse Core Ops, SparseCore 0:
  319.8 51.0 all-gather.6
  400.9 481.1 all-gather.8
  892.6 46.4 all-gather.10
